TPU v7x, 32 devices: a whole 2x2x4 slice. The times are simulated.
32 devices in a mesh: row: 4 (over z), col: 8 (over y, x, core).
Axes of the slice: x: 2, y: 2, z: 4, core: 2. Of those that a mesh axis runs over, the one named last changes fastest.
Arguments:
- flow_state: bfloat16 [8192, 256], P(('col', 'row')), may hold values from -6 to 6
- link_state: bfloat16 [4096, 256], P(('row', 'col')), may hold values from -6 to 6
- incidence: bfloat16 [4, 8, 24, 128, 128], P('row', 'col'), may hold values from -0.29882812 to 0.29882812
- tile_flow: int32 [4, 8, 24], P('row', 'col'), may hold values from 0 to 7
- tile_link: int32 [4, 8, 24], P('row', 'col'), may hold values from 0 to 7
- tile_live: int32 [4, 8, 24], P('row', 'col'), may hold values from 0 to 1, as said below
- link_gain: float32 [256], replicated, may hold values from 0.5 to 2
- link_agg_weight: bfloat16 [256, 256], replicated, may hold values from -0.375 to 0.375
- link_self_weight: bfloat16 [256, 256], replicated, may hold values from -0.375 to 0.375
- link_out_weight: bfloat16 [256, 256], replicated, may hold values from -0.375 to 0.375
- flow_gain: float32 [256], replicated, may hold values from 0.5 to 2
- flow_agg_weight: bfloat16 [256, 256], replicated, may hold values from -0.375 to 0.375
- flow_self_weight: bfloat16 [256, 256], replicated, may hold values from -0.375 to 0.375
- flow_out_weight: bfloat16 [256, 256], replicated, may hold values from -0.375 to 0.375
Outputs:
- link_next: bfloat16 [4096, 256], P(('row', 'col'))
- flow_next: bfloat16 [8192, 256], P(('col', 'row'))
Inputs may be any that keep to these rules, and one draw needn't show every extreme that they name: `tile_live`: in every draw some group pair has all 24 slots live; the number of live slots differs from pair to pair.
All inputs are finite; a program needn't handle non-finite values.
Results may differ from a plain program's by a relative error of at most 0.018.
Values may be sent and summed in bfloat16 or wider, within the bound.
A program may use at most 64 MiB of HBM per device.

v0:
```python
import jax
import jax.numpy as jnp
from jax import lax
from jax.sharding import PartitionSpec as P

H = 256
BS = 128


def state_update(totals, state, gain, agg_weight, self_weight, out_weight):
    scale = lax.rsqrt(jnp.mean(totals * totals, axis=-1, keepdims=True) + 1e-05)
    normed = (totals * scale * gain).astype(jnp.bfloat16)
    before = jnp.dot(normed, agg_weight, preferred_element_type=jnp.float32) + jnp.dot(
        state, self_weight, preferred_element_type=jnp.float32
    )
    hidden = jax.nn.silu(before).astype(jnp.bfloat16)
    return (
        state.astype(jnp.float32) + jnp.dot(hidden, out_weight, preferred_element_type=jnp.float32)
    ).astype(jnp.bfloat16)


def selector(targets, live_slots, block_count):
    select = (targets[None, :] == jnp.arange(block_count, dtype=jnp.int32)[:, None]).astype(
        jnp.float32
    )
    return select * live_slots.astype(jnp.float32)[None, :]


def on_device(
    flow_state,
    link_state,
    incidence,
    tile_flow,
    tile_link,
    tile_live,
    link_gain,
    link_agg_weight,
    link_self_weight,
    link_out_weight,
    flow_gain,
    flow_agg_weight,
    flow_self_weight,
    flow_out_weight,
):
    coefs = incidence[0, 0]
    flow_slots = tile_flow[0, 0]
    link_slots = tile_link[0, 0]
    live_slots = tile_live[0, 0]
    slot_count = coefs.shape[0]
    flow_blocks_here = flow_state.shape[0] // BS
    link_blocks_here = link_state.shape[0] // BS
    link_blocks = link_blocks_here * lax.axis_size("col")
    flow_group = lax.all_gather(flow_state, "row", axis=0, tiled=True)
    flow_blocks = flow_group.shape[0] // BS
    flow_pieces = jnp.take(flow_group.reshape(flow_blocks, BS, H), flow_slots, axis=0)
    link_terms = jnp.einsum(
        "tij,tih->tjh", coefs, flow_pieces, preferred_element_type=jnp.float32
    ).reshape(slot_count, BS * H)
    link_select = selector(link_slots, live_slots, link_blocks)
    chosen = link_select
    link_sum = lax.psum_scatter(
        jnp.dot(chosen, link_terms, precision=lax.Precision.HIGHEST).astype(jnp.bfloat16),
        "col",
        scatter_dimension=0,
        tiled=True,
    ).astype(jnp.float32)
    link_next = state_update(
        link_sum.reshape(link_blocks_here * BS, H),
        link_state,
        link_gain,
        link_agg_weight,
        link_self_weight,
        link_out_weight,
    )
    link_group = lax.all_gather(link_next, "col", axis=0, tiled=True)
    link_pieces = jnp.take(link_group.reshape(link_blocks, BS, H), link_slots, axis=0)
    flow_terms = jnp.einsum(
        "tij,tjh->tih", coefs, link_pieces, preferred_element_type=jnp.float32
    ).reshape(slot_count, BS * H)
    flow_select = selector(flow_slots, live_slots, flow_blocks)
    chosen = flow_select
    flow_sum = lax.psum_scatter(
        jnp.dot(chosen, flow_terms, precision=lax.Precision.HIGHEST).astype(jnp.bfloat16),
        "row",
        scatter_dimension=0,
        tiled=True,
    ).astype(jnp.float32)
    flow_next = state_update(
        flow_sum.reshape(flow_blocks_here * BS, H),
        flow_state,
        flow_gain,
        flow_agg_weight,
        flow_self_weight,
        flow_out_weight,
    )
    return (link_next, flow_next)


def solution(mesh):
    return jax.shard_map(
        on_device,
        mesh=mesh,
        in_specs=(
            P(("col", "row"), None),
            P(("row", "col"), None),
            P("row", "col", None, None, None),
            P("row", "col", None),
            P("row", "col", None),
            P("row", "col", None),
            P(),
            P(),
            P(),
            P(),
            P(),
            P(),
            P(),
            P(),
        ),
        out_specs=(P(("row", "col"), None), P(("col", "row"), None)),
        check_vma=False,
    )
```

profile of v0, /device:TPU:0, one launch (start us, length us, event | category | flops | bytes accessed | tf_op | source)
XLA Modules:
  0.0 165.6 jit_solution(4167647127550579348)
XLA Ops:
  7.2 0.0 copy-start
  7.2 0.0 all-reduce.5.cloned.1.call-start
  7.2 0.7 compare_and_fusion.1
  8.0 0.7 compare_select_fusion.1
  8.6 0.7 convert_bitcast_fusion
  9.3 17.6 %all_gather.6 = bf16[1024,256]{1,0:T(8,128)(2,1)S(1)} all-gather(bf16[256,256]{1,0:T(8,128)(2,1)} %param.16), channel_id=1, replica_groups=mesh['row'=4,'col'=8] {'row'}, dimensions={0}, use_global_device_ids=true | all-gather | bytes 655360 | tf_op jit(solution)/shard_map/all_gather | solution.py:53
  26.8 0.6 gather_fusion
  27.5 0.0 copy-done
  27.5 2.4 %convolution_bitcast_fusion.1 = f32[24,128,256]{1,2,0:T(8,128)} fusion(bf16[24,128,256]{2,1,0:T(8,128)(2,1)S(1)} %gather_fusion, pred[24]{0:T(512)(128)(4,1)S(1)} %compare_and_fusion.1, bf16[1,1,24,128,128]{4,3,2,1,0:T(8,128)(2,1)S(1)} %copy-done), kind=kOutput, calls=%fused_computation.5 | convolution fusion | flops 202113024 | bytes 5505048 | tf_op jit(solution)/shard_map/tij,tih->tjh/dot_general | solution.py:56
  29.9 3.6 %copy.26 = f32[3,8,128,256]{3,1,2,0:T(8,128)} copy(f32[3,8,128,256]{2,3,1,0:T(8,128)} %bitcast.41) | data formatting | bytes 6291456
  33.4 0.0 copy-done.7
  33.4 0.0 copy-start.5
  33.4 4.5 %convolution_convert_fusion.1 = bf16[8,32768]{1,0:T(8,128)(2,1)} fusion(f32[24,32768]{1,0:T(8,128)} %bitcast.40, f32[24]{0:T(128)S(1)} %convert_bitcast_fusion, s32[24]{0:T(128)S(1)} %bitcast.45), kind=kOutput, calls=%fused_computation.3 | convolution fusion | flops 75760000 | bytes 3670208 | tf_op jit(solution)/shard_map/dot_general | solution.py:62
  37.9 0.0 all-reduce.5.cloned.1.call-update
  37.9 0.0 all-reduce.7.cloned.1.call-start
  38.0 0.0 copy-done.15
  38.0 0.6 dynamic-slice
  38.6 55.8 %all-reduce.5.cloned.1.call-done = bf16[8,32768]{1,0:T(8,128)(2,1)} async-done(((bf16[8,32768]{1,0:T(8,128)(2,1)}), bf16[8,32768]{1,0:T(8,128)(2,1)}) %all-reduce.5.cloned.1.call-update) | async-done | bytes 524304
  94.4 2.1 %fusion.11 = f32[32768]{0:T(1024)S(1)} fusion(bf16[8,32768]{1,0:T(8,128)(2,1)} %all-reduce.5.cloned.1.call-done, u32[]{:T(128)} %bitcast.8), kind=kLoop, calls=%fused_computation.26 | loop fusion | flops 32768 | bytes 196612 | tf_op jit(solution)/shard_map/reshape | solution.py:68
  96.5 0.1 multiply_reduce_fusion.1
  96.7 0.0 copy-done.3
  96.7 0.0 copy-done.5
  96.7 0.2 fusion.15
  96.9 0.0 copy-done.9
  96.9 0.0 copy-done.10
  96.9 0.0 copy-done.13
  96.9 0.3 fusion.5
  97.2 0.0 copy-start.4
  97.2 9.1 %all_gather.7 = bf16[1024,256]{1,0:T(8,128)(2,1)S(1)} all-gather(bf16[128,256]{1,0:T(8,128)(2,1)S(1)} %fusion.5), channel_id=1, replica_groups=mesh['row'=4,'col'=8] {'col'}, dimensions={0}, use_global_device_ids=true | all-gather | bytes 589824 | tf_op jit(solution)/shard_map/all_gather | solution.py:75
  106.4 0.6 gather_fusion.1
  107.0 0.0 copy-done.4
  107.0 2.4 %convolution_bitcast_fusion = f32[24,128,256]{1,2,0:T(8,128)} fusion(bf16[24,128,256]{2,1,0:T(8,128)(2,1)S(1)} %gather_fusion.1, pred[24]{0:T(512)(128)(4,1)S(1)} %compare_and_fusion, bf16[1,1,24,128,128]{4,3,2,1,0:T(8,128)(2,1)S(1)} %copy-done), kind=kOutput, calls=%fused_computation.4 | convolution fusion | flops 202113024 | bytes 5505048 | tf_op jit(solution)/shard_map/tij,tjh->tih/dot_general | solution.py:77
  109.4 3.6 %copy.27 = f32[3,8,128,256]{3,1,2,0:T(8,128)} copy(f32[3,8,128,256]{2,3,1,0:T(8,128)} %bitcast.42) | data formatting | bytes 6291456
  113.0 0.0 copy-done.8
  113.0 4.4 %convolution_convert_fusion = bf16[8,32768]{1,0:T(8,128)(2,1)} fusion(f32[24,32768]{1,0:T(8,128)} %bitcast.39, s32[24]{0:T(128)S(1)} %bitcast.46, f32[24]{0:T(128)S(1)} %convert_bitcast_fusion), kind=kOutput, calls=%fused_computation.2 | convolution fusion | flops 75760000 | bytes 3670208 | tf_op jit(solution)/shard_map/dot_general | solution.py:83
  117.4 0.0 copy-start.12
  117.4 0.0 all-reduce.7.cloned.1.call-update
  117.4 0.0 copy-done.14
  117.5 0.6 dynamic-slice.2
  118.7 37.2 %all-reduce.7.cloned.1.call-done = bf16[8,32768]{1,0:T(8,128)(2,1)} async-done(((bf16[8,32768]{1,0:T(8,128)(2,1)}), bf16[8,32768]{1,0:T(8,128)(2,1)}) %all-reduce.7.cloned.1.call-update) | async-done | bytes 524304
  155.9 1.1 dynamic-slice_convert_fusion
  157.1 0.2 reshape.70
  157.3 0.1 multiply_reduce_fusion
  157.4 0.0 copy-done.1
  157.4 0.0 copy-done.6
  157.5 0.2 fusion.10
  157.7 0.0 copy-done.2
  157.7 1.0 fusion.4
  (21 shorter events, 0.1 us)
Async XLA Ops:
  7.2 20.3 %copy-start = (bf16[1,1,24,128,128]{4,3,2,1,0:T(8,128)(2,1)S(1)}, bf16[1,1,24,128,128]{4,3,2,1,0:T(8,128)(2,1)}, u32[]{:S(2)}) copy-start(bf16[1,1,24,128,128]{4,3,2,1,0:T(8,128)(2,1)} %param.18) | copy-start | bytes 2359300
  7.2 87.2 %all-reduce.5.cloned.1.call-start = ((), (), s32[]{:S(2)}) async-start(), calls=%async_computation | async-start | bytes 1048576
  29.9 3.6 %copy-start.7 = (s32[1,1,24]{2,1,0:T(1,128)S(1)}, s32[1,1,24]{2,1,0:T(1,128)}, u32[]{:S(2)}) copy-start(s32[1,1,24]{2,1,0:T(1,128)} %param.20) | copy-start | bytes 292
  33.4 4.6 %copy-start.15 = (u32[32]{0:T(128)S(1)}, u32[32]{0:T(128)}, u32[]{:S(2)}) copy-start(u32[32]{0:T(128)} %constant.33) | copy-start | bytes 388
  33.4 63.2 %copy-start.3 = (bf16[256,256]{1,0:T(8,128)(2,1)S(1)}, bf16[256,256]{1,0:T(8,128)(2,1)}, u32[]{:S(2)}) copy-start(bf16[256,256]{1,0:T(8,128)(2,1)} %param.23) | copy-start | bytes 393220
  33.4 63.2 %copy-start.5 = (f32[256]{0:T(256)S(1)}, f32[256]{0:T(256)}, u32[]{:S(2)}) copy-start(f32[256]{0:T(256)} %param.22) | copy-start | bytes 3076
  37.9 59.0 %copy-start.9 = (bf16[256,256]{1,0:T(8,128)(2,1)S(1)}, bf16[256,256]{1,0:T(8,128)(2,1)}, u32[]{:S(2)}) copy-start(bf16[256,256]{1,0:T(8,128)(2,1)} %param.25) | copy-start | bytes 393220
  37.9 59.0 %copy-start.10 = (bf16[256,256]{1,0:T(8,128)(2,1)S(1)}, bf16[256,256]{1,0:T(8,128)(2,1)}, u32[]{:S(2)}) copy-start(bf16[256,256]{1,0:T(8,128)(2,1)} %param.24) | copy-start | bytes 393220
  37.9 59.0 %copy-start.13 = (bf16[128,256]{1,0:T(8,128)(2,1)S(1)}, bf16[128,256]{1,0:T(8,128)(2,1)}, u32[]{:S(2)}) copy-start(bf16[128,256]{1,0:T(8,128)(2,1)} %param.17) | copy-start | bytes 196612
  37.9 118.0 %all-reduce.7.cloned.1.call-start = ((), (), s32[]{:S(2)}) async-start(), calls=%async_computation.1 | async-start | bytes 1048576
  97.2 9.8 %copy-start.4 = (bf16[128,256]{1,0:T(8,128)(2,1)}, bf16[128,256]{1,0:T(8,128)(2,1)S(1)}, u32[]{:S(2)}) copy-start(bf16[128,256]{1,0:T(8,128)(2,1)S(1)} %fusion.5) | copy-start | bytes 196612
  109.4 3.6 %copy-start.8 = (s32[1,1,24]{2,1,0:T(1,128)S(1)}, s32[1,1,24]{2,1,0:T(1,128)}, u32[]{:S(2)}) copy-start(s32[1,1,24]{2,1,0:T(1,128)} %param.19) | copy-start | bytes 292
  113.0 4.5 %copy-start.14 = (u32[32]{0:T(128)S(1)}, u32[32]{0:T(128)}, u32[]{:S(2)}) copy-start(u32[32]{0:T(128)} %constant.37) | copy-start | bytes 388
  117.4 40.0 %copy-start.1 = (bf16[256,256]{1,0:T(8,128)(2,1)S(1)}, bf16[256,256]{1,0:T(8,128)(2,1)}, u32[]{:S(2)}) copy-start(bf16[256,256]{1,0:T(8,128)(2,1)} %param.27) | copy-start | bytes 393220
  117.4 40.0 %copy-start.6 = (f32[256]{0:T(256)S(1)}, f32[256]{0:T(256)}, u32[]{:S(2)}) copy-start(f32[256]{0:T(256)} %param.26) | copy-start | bytes 3076
  117.4 40.3 %copy-start.2 = (bf16[256,256]{1,0:T(8,128)(2,1)S(1)}, bf16[256,256]{1,0:T(8,128)(2,1)}, u32[]{:S(2)}) copy-start(bf16[256,256]{1,0:T(8,128)(2,1)} %param.16) | copy-start | bytes 393220
  117.4 40.3 %copy-start.11 = (bf16[256,256]{1,0:T(8,128)(2,1)S(1)}, bf16[256,256]{1,0:T(8,128)(2,1)}, u32[]{:S(2)}) copy-start(bf16[256,256]{1,0:T(8,128)(2,1)} %param.29) | copy-start | bytes 393220
  117.4 40.3 %copy-start.12 = (bf16[256,256]{1,0:T(8,128)(2,1)S(1)}, bf16[256,256]{1,0:T(8,128)(2,1)}, u32[]{:S(2)}) copy-start(bf16[256,256]{1,0:T(8,128)(2,1)} %param.28) | copy-start | bytes 393220
Sparse Core Ops, SparseCore 0:
  38.1 56.2 all-reduce.4
  117.6 38.3 all-reduce.6
where the time goes:
time: 166 us
  waiting for transfers between devices  93 us (56%)
  blocking collectives  26.7 us (16%)
  matrix products  15.4 us (9%)
  between operations  14.9 us (9%)
  local copies, waits for them, and re-layouts  9.93 us (6%)
  other arithmetic  5.52 us (3%)
    unnamed x4, waiting for transfers between devices  93 us
    all_gather x1, blocking collectives, on_device(): flow_group = lax.all_gather(flow_state, 'row', axis=0, tiled=True)  17.6 us
    all_gather x1, blocking collectives, on_device(): link_group = lax.all_gather(link_next, 'col', axis=0, tiled=True)  9.13 us
    unnamed x36, local copies, waits for them, and re-layouts  8.37 us
    dot_general x1, matrix products, on_device(): jnp.dot(chosen, link_terms, precision=lax.Precision.HIGHEST)  4.46 us
    dot_general x1, matrix products, on_device(): jnp.dot(chosen, flow_terms, precision=lax.Precision.HIGHEST)  4.43 us
  transfers between devices with their start and end apart: 2, of which 2 were waited for; matrix products, arithmetic and copies ran while one was open for 1% of the time, Pallas kernels for 0%

commit v1 on v0

v1 whole, which is shorter than its diff:
```python
import functools

import jax
import jax.numpy as jnp
from jax import lax
from jax.experimental import pallas as pl
from jax.experimental.pallas import tpu as pltpu
from jax.sharding import PartitionSpec as P

H = 256
BS = 128
HALVES = 2
W = H // HALVES
MESH = pl.DeviceIdType.MESH


def sort_pairs(n):
    pairs = []
    p = 1
    while p < n:
        k = p
        while k >= 1:
            for j in range(k % p, n - k, 2 * k):
                for i in range(min(k, n - j - k)):
                    if (i + j) // (2 * p) == (i + j + k) // (2 * p):
                        pairs.append((i + j, i + j + k))
            k //= 2
        p *= 2
    return pairs


def order_slots(targets, sources, live, blocks, keys, ends):
    slots = targets.shape[2]
    held = []
    for s in range(slots):
        target = jnp.where(live[0, 0, s] == 1, targets[0, 0, s], blocks)
        held.append(target * 65536 + sources[0, 0, s] * 256 + s)
    for low, high in sort_pairs(slots):
        least, most = jnp.minimum(held[low], held[high]), jnp.maximum(held[low], held[high])
        held[low], held[high] = least, most
    keys[0] = jnp.int32(-1)
    for k in range(slots):
        keys[1 + k] = held[k]

    def count(b, carry):
        bound = (b + 1) * 65536
        below = jnp.int32(0)
        for k in range(slots):
            below = below + jnp.where(keys[1 + k] < bound, 1, 0)
        last = jnp.maximum(below - 1, 0)
        there = jnp.where(below > 0, jnp.where(lax.shift_right_logical(keys[1 + last], 16) == b, 1, 0), 0)
        ends[b] = last * 2 + there
        return carry

    lax.fori_loop(0, blocks, count, 0)


def segment_sums(slots, keys, ends, blocks, tile_of, source, sums, parts, half):
    unroll = 8 if slots % 8 == 0 else 1

    def steps(group, total):
        for inner in range(unroll):
            k = group * unroll + inner
            key = keys[1 + k]
            same = lax.shift_right_arithmetic(key, 16) == lax.shift_right_arithmetic(keys[k], 16)
            keep = jnp.where(same, 1.0, 0.0).astype(jnp.float32)
            piece = source[lax.shift_right_logical(key, 8) & 255]
            total = total * keep + jnp.dot(
                tile_of(k, key), piece, preferred_element_type=jnp.float32
            )
            sums[k] = total
        return total

    lax.fori_loop(0, slots // unroll, steps, jnp.zeros((BS, W), jnp.float32))

    def pick(b, carry):
        end = ends[b]
        there = jnp.where((end & 1) == 1, 1.0, 0.0).astype(jnp.float32)
        parts[half, b] = (sums[lax.shift_right_logical(end, 1)] * there).astype(jnp.bfloat16)
        return carry

    lax.fori_loop(0, blocks, pick, 0)


def updated(totals, state, own, gain, agg_weight, out_weight):
    square = sum(jnp.sum(t * t, axis=-1, keepdims=True) for t in totals)
    scale = lax.rsqrt(square * (1.0 / H) + 1e-05)
    before = own
    for half in range(HALVES):
        cut = slice(half * W, (half + 1) * W)
        normed = (totals[half] * scale * gain[:, cut]).astype(jnp.bfloat16)
        before = before + jnp.dot(normed, agg_weight[cut, :], preferred_element_type=jnp.float32)
    hidden = (before / (1.0 + jnp.exp(-before))).astype(jnp.bfloat16)
    return (
        state.astype(jnp.float32) + jnp.dot(hidden, out_weight[...], preferred_element_type=jnp.float32)
    ).astype(jnp.bfloat16)


def kernel(
    rows,
    cols,
    flow_state_hbm,
    link_state_hbm,
    coefs_hbm,
    link_agg_hbm,
    link_self_hbm,
    link_out_hbm,
    flow_agg_hbm,
    flow_self_hbm,
    flow_out_hbm,
    tile_flow,
    tile_link,
    tile_live,
    link_gain,
    flow_gain,
    link_next,
    flow_next,
    flow_state,
    link_state,
    coefs,
    link_agg,
    link_self,
    link_out,
    flow_agg,
    flow_self,
    flow_out,
    flows0,
    flows1,
    links0,
    links1,
    link_parts,
    link_in,
    flow_parts,
    flow_in,
    turned,
    sums,
    link_own,
    flow_own,
    link_keys,
    link_ends,
    flow_keys,
    flow_ends,
    send1,
    recv1,
    send2,
    recv2,
    send3,
    recv3,
    send4,
    recv4,
    own_sem,
    in_sem,
):
    flows, links = (flows0, flows1), (links0, links1)
    r, c = lax.axis_index("row"), lax.axis_index("col")
    slots = coefs.shape[2]
    fb, lb = flow_state.shape[0] // BS, link_state.shape[0] // BS
    flow_blocks, link_blocks = fb * rows, lb * cols

    def row_peer(t):
        return lax.rem(r + t, rows)

    def col_peer(t):
        return lax.rem(c + t, cols)

    def gather1(h, t):
        mine = flows[h].at[pl.ds(r * fb, fb)]
        return pltpu.make_async_remote_copy(
            src_ref=mine, dst_ref=mine, send_sem=send1.at[h, t], recv_sem=recv1.at[h, t],
            device_id=(row_peer(t), c), device_id_type=MESH,
        )

    def scatter2(h, t):
        peer = col_peer(t)
        return pltpu.make_async_remote_copy(
            src_ref=link_parts.at[h, pl.ds(peer * lb, lb)], dst_ref=link_in.at[h, t],
            send_sem=send2.at[h, t], recv_sem=recv2.at[h, t],
            device_id=(r, peer), device_id_type=MESH,
        )

    def gather3(h, t):
        mine = links[h].at[pl.ds(c * lb, lb)]
        return pltpu.make_async_remote_copy(
            src_ref=mine, dst_ref=mine, send_sem=send3.at[h, t], recv_sem=recv3.at[h, t],
            device_id=(r, col_peer(t)), device_id_type=MESH,
        )

    def scatter4(h, t):
        peer = row_peer(t)
        return pltpu.make_async_remote_copy(
            src_ref=flow_parts.at[h, pl.ds(peer * fb, fb)], dst_ref=flow_in.at[h, t],
            send_sem=send4.at[h, t], recv_sem=recv4.at[h, t],
            device_id=(peer, c), device_id_type=MESH,
        )

    row_steps, col_steps = range(1, rows), range(1, cols)
    barrier = pltpu.get_barrier_semaphore()
    for t in row_steps:
        pl.semaphore_signal(barrier, inc=1, device_id=(row_peer(t), c), device_id_type=MESH)
    for t in col_steps:
        pl.semaphore_signal(barrier, inc=1, device_id=(r, col_peer(t)), device_id_type=MESH)
    own_in = [
        pltpu.make_async_copy(
            flow_state_hbm.at[pl.ds(b * BS, BS), pl.ds(h * W, W)], flows[h].at[r * fb + b], own_sem.at[h, b]
        )
        for h in range(HALVES)
        for b in range(fb)
    ]
    pairs = (
        (coefs_hbm, coefs),
        (link_state_hbm, link_state),
        (link_self_hbm, link_self),
        (flow_state_hbm, flow_state),
        (flow_self_hbm, flow_self),
        (link_agg_hbm, link_agg),
        (link_out_hbm, link_out),
        (flow_agg_hbm, flow_agg),
        (flow_out_hbm, flow_out),
    )
    operands_in = [pltpu.make_async_copy(a, b, in_sem.at[n]) for n, (a, b) in enumerate(pairs)]
    for copy in own_in + operands_in:
        copy.start()
    for copy in own_in:
        copy.wait()
    pl.semaphore_wait(barrier, rows + cols - 2)

    for h in range(HALVES):
        for t in row_steps:
            gather1(h, t).start()

    order_slots(tile_link, tile_flow, tile_live, link_blocks, link_keys, link_ends)
    order_slots(tile_flow, tile_link, tile_live, flow_blocks, flow_keys, flow_ends)

    for copy in operands_in:
        copy.wait()

    def turn(k, carry):
        turned[k] = coefs[0, 0, link_keys[1 + k] & 255].T
        return carry

    lax.fori_loop(0, slots, turn, 0)
    link_own[...] = jnp.dot(link_state[...], link_self[...], preferred_element_type=jnp.float32)
    flow_own[...] = jnp.dot(flow_state[...], flow_self[...], preferred_element_type=jnp.float32)

    for h in range(HALVES):
        for t in row_steps:
            gather1(h, t).wait_recv()
        segment_sums(
            slots, link_keys, link_ends, link_blocks, lambda k, key: turned[k], flows[h], sums, link_parts, h
        )
        for t in col_steps:
            scatter2(h, t).start()

    totals = []
    for h in range(HALVES):
        total = link_parts[h, pl.ds(c * lb, lb)].astype(jnp.float32)
        for t in col_steps:
            scatter2(h, t).wait_recv()
            total = total + link_in[h, t].astype(jnp.float32)
        totals.append(total.reshape(lb * BS, W))
    fresh = updated(totals, link_state[...], link_own[...], link_gain, link_agg, link_out)
    for h in range(HALVES):
        for b in range(lb):
            links[h][c * lb + b] = fresh[b * BS : (b + 1) * BS, h * W : (h + 1) * W]
        for t in col_steps:
            gather3(h, t).start()
    link_next[...] = fresh

    for h in range(HALVES):
        for t in col_steps:
            gather3(h, t).wait_recv()
        segment_sums(
            slots, flow_keys, flow_ends, flow_blocks, lambda k, key: coefs[0, 0, key & 255], links[h], sums, flow_parts, h
        )
        for t in row_steps:
            scatter4(h, t).start()

    totals = []
    for h in range(HALVES):
        total = flow_parts[h, pl.ds(r * fb, fb)].astype(jnp.float32)
        for t in row_steps:
            scatter4(h, t).wait_recv()
            total = total + flow_in[h, t].astype(jnp.float32)
        totals.append(total.reshape(fb * BS, W))
    flow_next[...] = updated(totals, flow_state[...], flow_own[...], flow_gain, flow_agg, flow_out)

    for h in range(HALVES):
        for t in row_steps:
            gather1(h, t).wait_send()
            scatter4(h, t).wait_send()
        for t in col_steps:
            scatter2(h, t).wait_send()
            gather3(h, t).wait_send()


def on_device(
    rows,
    cols,
    flow_state,
    link_state,
    incidence,
    tile_flow,
    tile_link,
    tile_live,
    link_gain,
    link_agg_weight,
    link_self_weight,
    link_out_weight,
    flow_gain,
    flow_agg_weight,
    flow_self_weight,
    flow_out_weight,
):
    slots = incidence.shape[2]
    fb, lb = flow_state.shape[0] // BS, link_state.shape[0] // BS
    flow_blocks, link_blocks = fb * rows, lb * cols
    vmem = pl.BlockSpec(memory_space=pltpu.VMEM)
    hbm = pl.BlockSpec(memory_space=pl.ANY)
    smem = pl.BlockSpec(memory_space=pltpu.SMEM)
    bf16, f32, i32 = jnp.bfloat16, jnp.float32, jnp.int32
    dma = pltpu.SemaphoreType.DMA
    return pl.pallas_call(
        functools.partial(kernel, rows, cols),
        out_shape=(
            jax.ShapeDtypeStruct(link_state.shape, bf16),
            jax.ShapeDtypeStruct(flow_state.shape, bf16),
        ),
        in_specs=[hbm] * 9 + [smem] * 3 + [vmem] * 2,
        out_specs=(vmem, vmem),
        scratch_shapes=[
            pltpu.VMEM(flow_state.shape, bf16),
            pltpu.VMEM(link_state.shape, bf16),
            pltpu.VMEM(incidence.shape, bf16),
            *[pltpu.VMEM((H, H), bf16) for _ in range(6)],
            *[pltpu.VMEM((flow_blocks, BS, W), bf16) for _ in range(HALVES)],
            *[pltpu.VMEM((link_blocks, BS, W), bf16) for _ in range(HALVES)],
            pltpu.VMEM((HALVES, link_blocks, BS, W), bf16),
            pltpu.VMEM((HALVES, cols, lb, BS, W), bf16),
            pltpu.VMEM((HALVES, flow_blocks, BS, W), bf16),
            pltpu.VMEM((HALVES, rows, fb, BS, W), bf16),
            pltpu.VMEM((slots, BS, BS), bf16),
            pltpu.VMEM((slots, BS, W), f32),
            pltpu.VMEM((lb * BS, H), f32),
            pltpu.VMEM((fb * BS, H), f32),
            pltpu.SMEM((slots + 1,), i32),
            pltpu.SMEM((link_blocks,), i32),
            pltpu.SMEM((slots + 1,), i32),
            pltpu.SMEM((flow_blocks,), i32),
            dma((HALVES, rows)),
            dma((HALVES, rows)),
            dma((HALVES, cols)),
            dma((HALVES, cols)),
            dma((HALVES, cols)),
            dma((HALVES, cols)),
            dma((HALVES, rows)),
            dma((HALVES, rows)),
            dma((HALVES, fb)),
            dma((9,)),
        ],
        compiler_params=pltpu.CompilerParams(
            collective_id=0, has_side_effects=True, vmem_limit_bytes=40 * 1024 * 1024
        ),
        name="message_round",
    )(
        flow_state,
        link_state,
        incidence,
        link_agg_weight,
        link_self_weight,
        link_out_weight,
        flow_agg_weight,
        flow_self_weight,
        flow_out_weight,
        tile_flow,
        tile_link,
        tile_live,
        link_gain.reshape(1, H),
        flow_gain.reshape(1, H),
    )


def solution(mesh):
    return jax.shard_map(
        functools.partial(on_device, mesh.shape["row"], mesh.shape["col"]),
        mesh=mesh,
        in_specs=(
            P(("col", "row"), None),
            P(("row", "col"), None),
            P("row", "col", None, None, None),
            P("row", "col", None),
            P("row", "col", None),
            P("row", "col", None),
            P(),
            P(),
            P(),
            P(),
            P(),
            P(),
            P(),
            P(),
        ),
        out_specs=(P(("row", "col"), None), P(("col", "row"), None)),
        check_vma=False,
    )
```

time: 166 us -> 53.6 us (0.32)
  the two profiles are of different devices: /device:TPU:0 before, /device:TPU:1 now
where the time goes in v1:
time: 53.6 us; the launch traced here: 53.3 us
  Pallas kernels  42.3 us (79%)
  local copies, waits for them, and re-layouts  10.3 us (19%)
  between operations  0.7 us (1%)
    pallas_call x1, Pallas kernels, on_device(): pl.pallas_call(functools.partial(kernel, rows, cols), out_shape=(jax.Shap...  42.3 us
    unnamed x30, local copies, waits for them, and re-layouts  10.3 us

profile of v1, /device:TPU:1, one launch (start us, length us, event | category | flops | bytes accessed | tf_op | source)
XLA Modules:
  0.0 53.3 jit_solution(12391792838573470870)
XLA Ops:
  0.6 0.0 copy-start.10
  0.6 0.0 copy-start.12
  0.7 0.0 copy-start.13
  0.7 0.0 copy-start.9
  0.7 0.0 copy-start.11
  0.7 0.6 %copy-done.10 = f32[256]{0:T(256)S(1)} copy-done((f32[256]{0:T(256)S(1)}, f32[256]{0:T(256)}, u32[]{:S(2)}) %copy-start.10) | copy-done | bytes 1048
  1.3 0.0 copy-done.12
  1.3 0.0 copy-done.13
  1.3 0.0 copy-done.9
  1.4 0.0 copy-done.11
  1.4 0.0 copy-start
  1.4 1.1 %copy-done = bf16[1,1,24,128,128]{4,3,2,1,0:T(8,128)(2,1)S(1)} copy-done((bf16[1,1,24,128,128]{4,3,2,1,0:T(8,128)(2,1)S(1)}, bf16[1,1,24,128,128]{4,3,2,1,0:T(8,128)(2,1)}, u32[]{:S(2)}) %copy-start) | copy-done | bytes 786456
  2.5 0.0 copy-start.1
  2.5 0.9 %copy-done.1 = bf16[256,256]{1,0:T(8,128)(2,1)S(1)} copy-done((bf16[256,256]{1,0:T(8,128)(2,1)S(1)}, bf16[256,256]{1,0:T(8,128)(2,1)}, u32[]{:S(2)}) %copy-start.1) | copy-done | bytes 131096
  3.4 0.0 copy-start.2
  3.4 0.9 %copy-done.2 = bf16[256,256]{1,0:T(8,128)(2,1)S(1)} copy-done((bf16[256,256]{1,0:T(8,128)(2,1)S(1)}, bf16[256,256]{1,0:T(8,128)(2,1)}, u32[]{:S(2)}) %copy-start.2) | copy-done | bytes 131096
  4.3 0.0 copy-start.3
  4.3 0.9 %copy-done.3 = bf16[256,256]{1,0:T(8,128)(2,1)S(1)} copy-done((bf16[256,256]{1,0:T(8,128)(2,1)S(1)}, bf16[256,256]{1,0:T(8,128)(2,1)}, u32[]{:S(2)}) %copy-start.3) | copy-done | bytes 131096
  5.2 0.0 copy-start.4
  5.2 0.9 %copy-done.4 = bf16[256,256]{1,0:T(8,128)(2,1)S(1)} copy-done((bf16[256,256]{1,0:T(8,128)(2,1)S(1)}, bf16[256,256]{1,0:T(8,128)(2,1)}, u32[]{:S(2)}) %copy-start.4) | copy-done | bytes 131096
  6.1 0.0 copy-start.5
  6.1 0.9 %copy-done.5 = bf16[256,256]{1,0:T(8,128)(2,1)S(1)} copy-done((bf16[256,256]{1,0:T(8,128)(2,1)S(1)}, bf16[256,256]{1,0:T(8,128)(2,1)}, u32[]{:S(2)}) %copy-start.5) | copy-done | bytes 131096
  7.0 0.0 copy-start.6
  7.0 0.9 %copy-done.6 = bf16[256,256]{1,0:T(8,128)(2,1)S(1)} copy-done((bf16[256,256]{1,0:T(8,128)(2,1)S(1)}, bf16[256,256]{1,0:T(8,128)(2,1)}, u32[]{:S(2)}) %copy-start.6) | copy-done | bytes 131096
  7.9 0.0 copy-start.7
  7.9 0.9 %copy-done.7 = bf16[256,256]{1,0:T(8,128)(2,1)S(1)} copy-done((bf16[256,256]{1,0:T(8,128)(2,1)S(1)}, bf16[256,256]{1,0:T(8,128)(2,1)}, u32[]{:S(2)}) %copy-start.7) | copy-done | bytes 131096
  8.8 0.0 copy-start.8
  8.8 0.8 %copy-done.8 = bf16[128,256]{1,0:T(8,128)(2,1)S(1)} copy-done((bf16[128,256]{1,0:T(8,128)(2,1)S(1)}, bf16[128,256]{1,0:T(8,128)(2,1)}, u32[]{:S(2)}) %copy-start.8) | copy-done | bytes 65560
  9.7 42.3 %message_round.1 = (bf16[128,256]{1,0:T(8,128)(2,1)S(1)}, bf16[256,256]{1,0:T(8,128)(2,1)S(1)}) custom-call(bf16[256,256]{1,0:T(8,128)(2,1)S(1)} %copy-done.1, bf16[128,256]{1,0:T(8,128)(2,1)S(1)} %copy-done.8, bf16[1,1,24,128,128]{4,3,2,1,0:T(8,128)(2,1)S(1)} %copy-done, bf16[256,256]{1,0:T(8,128)(2,1)S(1)} %copy-done.2, bf16[256,256]{1,0:T(8,128)(2,1)S(1)} %copy-done.3, ...), custom_call_target="tpu_custom_call" | custom-call | tf_op jit(solution)/shard_map/message_round/pallas_call | solution.py:322
  52.0 0.6 %copy.18 = bf16[128,256]{1,0:T(8,128)(2,1)} copy(bf16[128,256]{1,0:T(8,128)(2,1)S(1)} %get-tuple-element.4) | data formatting | bytes 131072
  52.6 0.7 %copy.19 = bf16[256,256]{1,0:T(8,128)(2,1)} copy(bf16[256,256]{1,0:T(8,128)(2,1)S(1)} %get-tuple-element.5) | data formatting | bytes 262144
Async XLA Ops:
  0.6 0.7 %copy-start.10 = (f32[256]{0:T(256)S(1)}, f32[256]{0:T(256)}, u32[]{:S(2)}) copy-start(f32[256]{0:T(256)} %param.24) | copy-start | bytes 3076
  0.6 0.7 %copy-start.12 = (s32[1,1,24]{2,1,0:T(1,128)S(1)}, s32[1,1,24]{2,1,0:T(1,128)}, u32[]{:S(2)}) copy-start(s32[1,1,24]{2,1,0:T(1,128)} %tile_link.1) | copy-start | bytes 292
  0.7 0.7 %copy-start.13 = (s32[1,1,24]{2,1,0:T(1,128)S(1)}, s32[1,1,24]{2,1,0:T(1,128)}, u32[]{:S(2)}) copy-start(s32[1,1,24]{2,1,0:T(1,128)} %tile_live.1) | copy-start | bytes 292
  0.7 0.7 %copy-start.9 = (f32[256]{0:T(256)S(1)}, f32[256]{0:T(256)}, u32[]{:S(2)}) copy-start(f32[256]{0:T(256)} %param.20) | copy-start | bytes 3076
  0.7 0.7 %copy-start.11 = (s32[1,1,24]{2,1,0:T(1,128)S(1)}, s32[1,1,24]{2,1,0:T(1,128)}, u32[]{:S(2)}) copy-start(s32[1,1,24]{2,1,0:T(1,128)} %tile_flow.1) | copy-start | bytes 292
  1.4 1.1 %copy-start = (bf16[1,1,24,128,128]{4,3,2,1,0:T(8,128)(2,1)S(1)}, bf16[1,1,24,128,128]{4,3,2,1,0:T(8,128)(2,1)}, u32[]{:S(2)}) copy-start(bf16[1,1,24,128,128]{4,3,2,1,0:T(8,128)(2,1)} %coefs_hbm.1) | copy-start | bytes 2359300
  2.5 0.9 %copy-start.1 = (bf16[256,256]{1,0:T(8,128)(2,1)S(1)}, bf16[256,256]{1,0:T(8,128)(2,1)}, u32[]{:S(2)}) copy-start(bf16[256,256]{1,0:T(8,128)(2,1)} %flow_state_hbm.1) | copy-start | bytes 393220
  3.4 0.9 %copy-start.2 = (bf16[256,256]{1,0:T(8,128)(2,1)S(1)}, bf16[256,256]{1,0:T(8,128)(2,1)}, u32[]{:S(2)}) copy-start(bf16[256,256]{1,0:T(8,128)(2,1)} %link_agg_hbm.1) | copy-start | bytes 393220
  4.3 0.9 %copy-start.3 = (bf16[256,256]{1,0:T(8,128)(2,1)S(1)}, bf16[256,256]{1,0:T(8,128)(2,1)}, u32[]{:S(2)}) copy-start(bf16[256,256]{1,0:T(8,128)(2,1)} %link_self_hbm.1) | copy-start | bytes 393220
  5.2 0.9 %copy-start.4 = (bf16[256,256]{1,0:T(8,128)(2,1)S(1)}, bf16[256,256]{1,0:T(8,128)(2,1)}, u32[]{:S(2)}) copy-start(bf16[256,256]{1,0:T(8,128)(2,1)} %link_out_hbm.1) | copy-start | bytes 393220
  6.1 0.9 %copy-start.5 = (bf16[256,256]{1,0:T(8,128)(2,1)S(1)}, bf16[256,256]{1,0:T(8,128)(2,1)}, u32[]{:S(2)}) copy-start(bf16[256,256]{1,0:T(8,128)(2,1)} %flow_agg_hbm.1) | copy-start | bytes 393220
  7.0 0.9 %copy-start.6 = (bf16[256,256]{1,0:T(8,128)(2,1)S(1)}, bf16[256,256]{1,0:T(8,128)(2,1)}, u32[]{:S(2)}) copy-start(bf16[256,256]{1,0:T(8,128)(2,1)} %flow_self_hbm.1) | copy-start | bytes 393220
  7.9 0.9 %copy-start.7 = (bf16[256,256]{1,0:T(8,128)(2,1)S(1)}, bf16[256,256]{1,0:T(8,128)(2,1)}, u32[]{:S(2)}) copy-start(bf16[256,256]{1,0:T(8,128)(2,1)} %flow_out_hbm.1) | copy-start | bytes 393220
  8.8 0.8 %copy-start.8 = (bf16[128,256]{1,0:T(8,128)(2,1)S(1)}, bf16[128,256]{1,0:T(8,128)(2,1)}, u32[]{:S(2)}) copy-start(bf16[128,256]{1,0:T(8,128)(2,1)} %link_state_hbm.1) | copy-start | bytes 196612

commit v2 on v1

--- a/solution.py
+++ b/solution.py
@@ -108,11 +108,11 @@
     flow_agg_hbm,
     flow_self_hbm,
     flow_out_hbm,
-    tile_flow,
-    tile_link,
-    tile_live,
-    link_gain,
-    flow_gain,
+    tile_flow_hbm,
+    tile_link_hbm,
+    tile_live_hbm,
+    link_gain_hbm,
+    flow_gain_hbm,
     link_next,
     flow_next,
     flow_state,
@@ -124,6 +124,11 @@
     flow_agg,
     flow_self,
     flow_out,
+    link_gain,
+    flow_gain,
+    tile_flow,
+    tile_link,
+    tile_live,
     flows0,
     flows1,
     links0,
@@ -150,6 +155,10 @@
     recv4,
     own_sem,
     in_sem,
+    relay_in,
+    relay_send1,
+    relay_send4,
+    relay_recv4,
 ):
     flows, links = (flows0, flows1), (links0, links1)
     r, c = lax.axis_index("row"), lax.axis_index("col")
@@ -193,7 +202,49 @@
             device_id=(peer, c), device_id_type=MESH,
         )
 
-    row_steps, col_steps = range(1, rows), range(1, cols)
+    last = rows - 1
+    ways = ((0, 1, rows - 2, last), (last, last - 1, 1, 0)) if rows > 2 else ()
+
+    def relay1(h, way):
+        begin, _, near, end = ways[way]
+        shard = flows[h].at[pl.ds(begin * fb, fb)]
+        return pltpu.make_async_remote_copy(
+            src_ref=shard, dst_ref=shard, send_sem=relay_send1.at[h, way],
+            recv_sem=recv1.at[h, (end - begin) % rows],
+            device_id=(end, c), device_id_type=MESH,
+        )
+
+    def relay4(h, way):
+        begin, near, _, end = ways[way]
+        return pltpu.make_async_remote_copy(
+            src_ref=flow_parts.at[h, pl.ds(end * fb, fb)], dst_ref=relay_in.at[h, way],
+            send_sem=relay_send4.at[h, way], recv_sem=relay_recv4.at[h, way],
+            device_id=(near, c), device_id_type=MESH,
+        )
+
+    def unless(places, act):
+        if not places:
+            act()
+            return
+        free = r != places[0]
+        for place in places[1:]:
+            free = jnp.logical_and(free, r != place)
+        pl.when(free)(act)
+
+    def ends_of(t):
+        return [begin for begin, _, _, end in ways if (end - begin) % rows == t]
+
+    def met(t):
+        return [end for begin, _, _, end in ways if (end - begin) % rows == t]
+
+    def passed1(t):
+        return [near for begin, _, near, _ in ways if (near - begin) % rows == t]
+
+    def joined4(t):
+        return [near for _, near, _, end in ways if (end - near) % rows == t]
+
+    row_steps = sorted(range(1, rows), key=lambda t: (-min(t, rows - t), t))
+    col_steps = range(1, cols)
     barrier = pltpu.get_barrier_semaphore()
     for t in row_steps:
         pl.semaphore_signal(barrier, inc=1, device_id=(row_peer(t), c), device_id_type=MESH)
@@ -216,9 +267,17 @@
         (link_out_hbm, link_out),
         (flow_agg_hbm, flow_agg),
         (flow_out_hbm, flow_out),
+        (link_gain_hbm, link_gain),
+        (flow_gain_hbm, flow_gain),
     )
+    tables = (
+        (tile_flow_hbm, tile_flow),
+        (tile_link_hbm, tile_link),
+        (tile_live_hbm, tile_live),
+    )
+    tables_in = [pltpu.make_async_copy(a, b, in_sem.at[len(pairs) + n]) for n, (a, b) in enumerate(tables)]
     operands_in = [pltpu.make_async_copy(a, b, in_sem.at[n]) for n, (a, b) in enumerate(pairs)]
-    for copy in own_in + operands_in:
+    for copy in own_in + tables_in + operands_in:
         copy.start()
     for copy in own_in:
         copy.wait()
@@ -226,8 +285,16 @@
 
     for h in range(HALVES):
         for t in row_steps:
-            gather1(h, t).start()
-
+            unless(ends_of(t), lambda: gather1(h, t).start())
+    for h in range(HALVES):
+        for way, (begin, _, _, end) in enumerate(ways):
+
+            @pl.when(r == end)
+            def _():
+                flow_in[h, (end - begin) % rows] = jnp.zeros((fb, BS, W), jnp.bfloat16)
+
+    for copy in tables_in:
+        copy.wait()
     order_slots(tile_link, tile_flow, tile_live, link_blocks, link_keys, link_ends)
     order_slots(tile_flow, tile_link, tile_live, flow_blocks, flow_keys, flow_ends)
 
@@ -243,8 +310,16 @@
     flow_own[...] = jnp.dot(flow_state[...], flow_self[...], preferred_element_type=jnp.float32)
 
     for h in range(HALVES):
+        for way, (begin, _, near, _) in enumerate(ways):
+
+            @pl.when(r == near)
+            def _():
+                gather1(h, (near - begin) % rows).wait_recv()
+                relay1(h, way).start()
+
+    for h in range(HALVES):
         for t in row_steps:
-            gather1(h, t).wait_recv()
+            unless(passed1(t), lambda: gather1(h, t).wait_recv())
         segment_sums(
             slots, link_keys, link_ends, link_blocks, lambda k, key: turned[k], flows[h], sums, link_parts, h
         )
@@ -272,22 +347,37 @@
         segment_sums(
             slots, flow_keys, flow_ends, flow_blocks, lambda k, key: coefs[0, 0, key & 255], links[h], sums, flow_parts, h
         )
+        for way, (begin, _, _, _) in enumerate(ways):
+            pl.when(r == begin)(lambda: relay4(h, way).start())
         for t in row_steps:
-            scatter4(h, t).start()
+            unless(ends_of(t) + joined4(t), lambda: scatter4(h, t).start())
+    for h in range(HALVES):
+        for way, (_, near, _, end) in enumerate(ways):
+
+            @pl.when(r == near)
+            def _():
+                relay4(h, way).wait_recv()
+                part = flow_parts[h, pl.ds(end * fb, fb)].astype(jnp.float32)
+                part = part + relay_in[h, way].astype(jnp.float32)
+                flow_parts[h, pl.ds(end * fb, fb)] = part.astype(jnp.bfloat16)
+                scatter4(h, (end - near) % rows).start()
 
     totals = []
     for h in range(HALVES):
         total = flow_parts[h, pl.ds(r * fb, fb)].astype(jnp.float32)
         for t in row_steps:
-            scatter4(h, t).wait_recv()
+            unless(met(t), lambda: scatter4(h, t).wait_recv())
             total = total + flow_in[h, t].astype(jnp.float32)
         totals.append(total.reshape(fb * BS, W))
     flow_next[...] = updated(totals, flow_state[...], flow_own[...], flow_gain, flow_agg, flow_out)
 
     for h in range(HALVES):
         for t in row_steps:
-            gather1(h, t).wait_send()
-            scatter4(h, t).wait_send()
+            unless(ends_of(t), lambda: gather1(h, t).wait_send())
+            unless(ends_of(t), lambda: scatter4(h, t).wait_send())
+        for way, (begin, _, near, _) in enumerate(ways):
+            pl.when(r == near)(lambda: relay1(h, way).wait_send())
+            pl.when(r == begin)(lambda: relay4(h, way).wait_send())
         for t in col_steps:
             scatter2(h, t).wait_send()
             gather3(h, t).wait_send()
@@ -315,8 +405,7 @@
     fb, lb = flow_state.shape[0] // BS, link_state.shape[0] // BS
     flow_blocks, link_blocks = fb * rows, lb * cols
     vmem = pl.BlockSpec(memory_space=pltpu.VMEM)
-    hbm = pl.BlockSpec(memory_space=pl.ANY)
-    smem = pl.BlockSpec(memory_space=pltpu.SMEM)
+    hbm = pl.BlockSpec(memory_space=pltpu.HBM)
     bf16, f32, i32 = jnp.bfloat16, jnp.float32, jnp.int32
     dma = pltpu.SemaphoreType.DMA
     return pl.pallas_call(
@@ -325,13 +414,15 @@
             jax.ShapeDtypeStruct(link_state.shape, bf16),
             jax.ShapeDtypeStruct(flow_state.shape, bf16),
         ),
-        in_specs=[hbm] * 9 + [smem] * 3 + [vmem] * 2,
+        in_specs=[hbm] * 14,
         out_specs=(vmem, vmem),
         scratch_shapes=[
             pltpu.VMEM(flow_state.shape, bf16),
             pltpu.VMEM(link_state.shape, bf16),
             pltpu.VMEM(incidence.shape, bf16),
             *[pltpu.VMEM((H, H), bf16) for _ in range(6)],
+            *[pltpu.VMEM((1, H), f32) for _ in range(2)],
+            *[pltpu.SMEM((1, 1, slots), i32) for _ in range(3)],
             *[pltpu.VMEM((flow_blocks, BS, W), bf16) for _ in range(HALVES)],
             *[pltpu.VMEM((link_blocks, BS, W), bf16) for _ in range(HALVES)],
             pltpu.VMEM((HALVES, link_blocks, BS, W), bf16),
@@ -355,10 +446,14 @@
             dma((HALVES, rows)),
             dma((HALVES, rows)),
             dma((HALVES, fb)),
-            dma((9,)),
+            dma((14,)),
+            pltpu.VMEM((HALVES, 2, fb, BS, W), bf16),
+            dma((HALVES, 2)),
+            dma((HALVES, 2)),
+            dma((HALVES, 2)),
         ],
         compiler_params=pltpu.CompilerParams(
-            collective_id=0, has_side_effects=True, vmem_limit_bytes=40 * 1024 * 1024
+            collective_id=0, has_side_effects=True, vmem_limit_bytes=60 * 1024 * 1024
         ),
         name="message_round",
     )(

time: 53.6 us -> 43.8 us (0.82)
  the two profiles are of different devices: /device:TPU:1 before, /device:TPU:0 now
where the time goes in v2:
time: 43.8 us; the launch traced here: 43.6 us
  Pallas kernels  40.8 us (93%)
  local copies, waits for them, and re-layouts  2.17 us (5%)
  between operations  0.65 us (1%)
    pallas_call x1, Pallas kernels, on_device(): pl.pallas_call(functools.partial(kernel, rows, cols), out_shape=(jax.Shap...  40.8 us
    unnamed x4, local copies, waits for them, and re-layouts  2.17 us

profile of v2, /device:TPU:0, one launch (start us, length us, event | category | flops | bytes accessed | tf_op | source)
XLA Modules:
  0.0 43.6 jit_solution(14382273269524593819)
XLA Ops:
  0.6 40.8 %message_round.1 = (bf16[128,256]{1,0:T(8,128)(2,1)}, bf16[256,256]{1,0:T(8,128)(2,1)}) custom-call(bf16[256,256]{1,0:T(8,128)(2,1)} %flow_state_hbm.1, bf16[128,256]{1,0:T(8,128)(2,1)} %link_state_hbm.1, bf16[1,1,24,128,128]{4,3,2,1,0:T(8,128)(2,1)} %coefs_hbm.1, bf16[256,256]{1,0:T(8,128)(2,1)} %link_agg_hbm.1, bf16[256,256]{1,0:T(8,128)(2,1)} %link_self_hbm.1, ...), custom_call_target="tpu_custom_call" | custom-call | tf_op jit(solution)/shard_map/message_round/pallas_call | solution.py:411
  41.5 0.0 copy-start
  41.5 1.5 %copy.18 = bf16[128,256]{1,0:T(8,128)(2,1)} copy(bf16[128,256]{1,0:T(8,128)(2,1)} %get-tuple-element.4) | data formatting | bytes 131072
  43.0 0.0 copy-done
  43.0 0.7 %copy.19 = bf16[256,256]{1,0:T(8,128)(2,1)} copy(bf16[256,256]{1,0:T(8,128)(2,1)S(1)} %copy-done) | data formatting | bytes 262144
Async XLA Ops:
  41.5 1.5 %copy-start = (bf16[256,256]{1,0:T(8,128)(2,1)S(1)}, bf16[256,256]{1,0:T(8,128)(2,1)}, u32[]{:S(2)}) copy-start(bf16[256,256]{1,0:T(8,128)(2,1)} %get-tuple-element.5) | copy-start | bytes 393220

commit v3 on v2

--- a/solution.py
+++ b/solution.py
@@ -283,9 +283,8 @@
         copy.wait()
     pl.semaphore_wait(barrier, rows + cols - 2)
 
-    for h in range(HALVES):
-        for t in row_steps:
-            unless(ends_of(t), lambda: gather1(h, t).start())
+    for t in row_steps:
+        unless(ends_of(t), lambda: gather1(0, t).start())
     for h in range(HALVES):
         for way, (begin, _, _, end) in enumerate(ways):
 
@@ -298,6 +297,11 @@
     order_slots(tile_link, tile_flow, tile_live, link_blocks, link_keys, link_ends)
     order_slots(tile_flow, tile_link, tile_live, flow_blocks, flow_keys, flow_ends)
 
+    for h in range(1, HALVES):
+        for t in row_steps:
+            unless(ends_of(t), lambda: gather1(h - 1, t).wait_send())
+        for t in row_steps:
+            unless(ends_of(t), lambda: gather1(h, t).start())
     for copy in operands_in:
         copy.wait()
 
@@ -334,12 +338,15 @@
             total = total + link_in[h, t].astype(jnp.float32)
         totals.append(total.reshape(lb * BS, W))
     fresh = updated(totals, link_state[...], link_own[...], link_gain, link_agg, link_out)
+    link_next[...] = fresh
     for h in range(HALVES):
         for b in range(lb):
             links[h][c * lb + b] = fresh[b * BS : (b + 1) * BS, h * W : (h + 1) * W]
         for t in col_steps:
+            if h > 0:
+                gather3(h - 1, t).wait_send()
+        for t in col_steps:
             gather3(h, t).start()
-    link_next[...] = fresh
 
     for h in range(HALVES):
         for t in col_steps:
@@ -373,14 +380,16 @@
 
     for h in range(HALVES):
         for t in row_steps:
-            unless(ends_of(t), lambda: gather1(h, t).wait_send())
+            if h == HALVES - 1:
+                unless(ends_of(t), lambda: gather1(h, t).wait_send())
             unless(ends_of(t), lambda: scatter4(h, t).wait_send())
         for way, (begin, _, near, _) in enumerate(ways):
             pl.when(r == near)(lambda: relay1(h, way).wait_send())
             pl.when(r == begin)(lambda: relay4(h, way).wait_send())
         for t in col_steps:
             scatter2(h, t).wait_send()
-            gather3(h, t).wait_send()
+            if h == HALVES - 1:
+                gather3(h, t).wait_send()
 
 
 def on_device(

time: 43.8 us -> 45.9 us (1.048)
  Pallas kernels: 40.8 us -> 42.9 us
    pallas_call x1, Pallas kernels: 40.8 us -> 42.9 us  [on_device(): pl.pallas_call(functools.partial(kernel, rows, cols), out_shape=(jax.Shap...]
where the time goes in v3:
time: 45.9 us; the launch traced here: 45.7 us
  Pallas kernels  42.9 us (93%)
  local copies, waits for them, and re-layouts  2.17 us (5%)
  between operations  0.65 us (1%)
    pallas_call x1, Pallas kernels, on_device(): pl.pallas_call(functools.partial(kernel, rows, cols), out_shape=(jax.Shap...  42.9 us
    unnamed x4, local copies, waits for them, and re-layouts  2.17 us

profile of v3, /device:TPU:0, one launch (start us, length us, event | category | flops | bytes accessed | tf_op | source)
XLA Modules:
  0.0 45.7 jit_solution(11976736479459468365)
XLA Ops:
  0.6 42.9 %message_round.1 = (bf16[128,256]{1,0:T(8,128)(2,1)}, bf16[256,256]{1,0:T(8,128)(2,1)}) custom-call(bf16[256,256]{1,0:T(8,128)(2,1)} %flow_state_hbm.1, bf16[128,256]{1,0:T(8,128)(2,1)} %link_state_hbm.1, bf16[1,1,24,128,128]{4,3,2,1,0:T(8,128)(2,1)} %coefs_hbm.1, bf16[256,256]{1,0:T(8,128)(2,1)} %link_agg_hbm.1, bf16[256,256]{1,0:T(8,128)(2,1)} %link_self_hbm.1, ...), custom_call_target="tpu_custom_call" | custom-call | tf_op jit(solution)/shard_map/message_round/pallas_call | solution.py:420
  43.5 0.0 copy-start
  43.5 1.5 %copy.18 = bf16[128,256]{1,0:T(8,128)(2,1)} copy(bf16[128,256]{1,0:T(8,128)(2,1)} %get-tuple-element.4) | data formatting | bytes 131072
  45.0 0.0 copy-done
  45.1 0.7 %copy.19 = bf16[256,256]{1,0:T(8,128)(2,1)} copy(bf16[256,256]{1,0:T(8,128)(2,1)S(1)} %copy-done) | data formatting | bytes 262144
Async XLA Ops:
  43.5 1.5 %copy-start = (bf16[256,256]{1,0:T(8,128)(2,1)S(1)}, bf16[256,256]{1,0:T(8,128)(2,1)}, u32[]{:S(2)}) copy-start(bf16[256,256]{1,0:T(8,128)(2,1)} %get-tuple-element.5) | copy-start | bytes 393220

commit v4 on v2

--- a/solution.py
+++ b/solution.py
@@ -82,14 +82,17 @@
     lax.fori_loop(0, blocks, pick, 0)
 
 
-def updated(totals, state, own, gain, agg_weight, out_weight):
-    square = sum(jnp.sum(t * t, axis=-1, keepdims=True) for t in totals)
+def gained(total, half, gain, agg_weight):
+    cut = slice(half * W, (half + 1) * W)
+    product = jnp.dot(
+        (total * gain[:, cut]).astype(jnp.bfloat16), agg_weight[cut, :], preferred_element_type=jnp.float32
+    )
+    return jnp.sum(total * total, axis=-1, keepdims=True), product
+
+
+def updated(square, product, state, own, out_weight):
     scale = lax.rsqrt(square * (1.0 / H) + 1e-05)
-    before = own
-    for half in range(HALVES):
-        cut = slice(half * W, (half + 1) * W)
-        normed = (totals[half] * scale * gain[:, cut]).astype(jnp.bfloat16)
-        before = before + jnp.dot(normed, agg_weight[cut, :], preferred_element_type=jnp.float32)
+    before = own + product * scale
     hidden = (before / (1.0 + jnp.exp(-before))).astype(jnp.bfloat16)
     return (
         state.astype(jnp.float32) + jnp.dot(hidden, out_weight[...], preferred_element_type=jnp.float32)
@@ -194,6 +197,16 @@
             device_id=(r, col_peer(t)), device_id_type=MESH,
         )
 
+    partner = c + 1 - 2 * lax.rem(c, 2)
+    chip_steps = range(2, cols, 2)
+
+    def relay3(h, t):
+        shard = links[h].at[pl.ds(lax.rem(c + cols - t, cols) * lb, lb)]
+        return pltpu.make_async_remote_copy(
+            src_ref=shard, dst_ref=shard, send_sem=send3.at[h, t + 1], recv_sem=recv3.at[h, t + 1],
+            device_id=(r, partner), device_id_type=MESH,
+        )
+
     def scatter4(h, t):
         peer = row_peer(t)
         return pltpu.make_async_remote_copy(
@@ -301,15 +314,7 @@
     for copy in operands_in:
         copy.wait()
 
-    def turn(k, carry):
-        turned[k] = coefs[0, 0, link_keys[1 + k] & 255].T
-        return carry
-
-    lax.fori_loop(0, slots, turn, 0)
-    link_own[...] = jnp.dot(link_state[...], link_self[...], preferred_element_type=jnp.float32)
-    flow_own[...] = jnp.dot(flow_state[...], flow_self[...], preferred_element_type=jnp.float32)
-
-    for h in range(HALVES):
+    def pass_on(h):
         for way, (begin, _, near, _) in enumerate(ways):
 
             @pl.when(r == near)
@@ -317,6 +322,18 @@
                 gather1(h, (near - begin) % rows).wait_recv()
                 relay1(h, way).start()
 
+    pass_on(0)
+
+    def turn(k, carry):
+        turned[k] = coefs[0, 0, link_keys[1 + k] & 255].T
+        return carry
+
+    lax.fori_loop(0, slots, turn, 0)
+    link_own[...] = jnp.dot(link_state[...], link_self[...], preferred_element_type=jnp.float32)
+    flow_own[...] = jnp.dot(flow_state[...], flow_self[...], preferred_element_type=jnp.float32)
+
+    pass_on(1)
+
     for h in range(HALVES):
         for t in row_steps:
             unless(passed1(t), lambda: gather1(h, t).wait_recv())
@@ -332,18 +349,24 @@
         for t in col_steps:
             scatter2(h, t).wait_recv()
             total = total + link_in[h, t].astype(jnp.float32)
-        totals.append(total.reshape(lb * BS, W))
-    fresh = updated(totals, link_state[...], link_own[...], link_gain, link_agg, link_out)
+        square, product = gained(total.reshape(lb * BS, W), h, link_gain, link_agg)
+        totals.append((square, product))
+    square, product = (sum(terms[1:], terms[0]) for terms in zip(*totals))
+    fresh = updated(square, product, link_state[...], link_own[...], link_out)
     for h in range(HALVES):
         for b in range(lb):
             links[h][c * lb + b] = fresh[b * BS : (b + 1) * BS, h * W : (h + 1) * W]
-        for t in col_steps:
+        for t in chip_steps:
             gather3(h, t).start()
+        relay3(h, 0).start()
     link_next[...] = fresh
 
     for h in range(HALVES):
-        for t in col_steps:
+        for t in chip_steps:
             gather3(h, t).wait_recv()
+            relay3(h, t).start()
+        for t in (0, *chip_steps):
+            relay3(h, t).wait_recv()
         segment_sums(
             slots, flow_keys, flow_ends, flow_blocks, lambda k, key: coefs[0, 0, key & 255], links[h], sums, flow_parts, h
         )
@@ -368,8 +391,10 @@
         for t in row_steps:
             unless(met(t), lambda: scatter4(h, t).wait_recv())
             total = total + flow_in[h, t].astype(jnp.float32)
-        totals.append(total.reshape(fb * BS, W))
-    flow_next[...] = updated(totals, flow_state[...], flow_own[...], flow_gain, flow_agg, flow_out)
+        square, product = gained(total.reshape(fb * BS, W), h, flow_gain, flow_agg)
+        totals.append((square, product))
+    square, product = (sum(terms[1:], terms[0]) for terms in zip(*totals))
+    flow_next[...] = updated(square, product, flow_state[...], flow_own[...], flow_out)
 
     for h in range(HALVES):
         for t in row_steps:
@@ -380,7 +405,10 @@
             pl.when(r == begin)(lambda: relay4(h, way).wait_send())
         for t in col_steps:
             scatter2(h, t).wait_send()
+        for t in chip_steps:
             gather3(h, t).wait_send()
+        for t in (0, *chip_steps):
+            relay3(h, t).wait_send()
 
 
 def on_device(

time: 43.8 us -> 43.6 us (level)
  no operation moved by 1% of the time
where the time goes in v4:
time: 43.6 us; the launch traced here: 43.4 us
  Pallas kernels  40.6 us (93%)
  local copies, waits for them, and re-layouts  2.17 us (5%)
  between operations  0.65 us (1%)
    pallas_call x1, Pallas kernels, on_device(): pl.pallas_call(functools.partial(kernel, rows, cols), out_shape=(jax.Shap...  40.6 us
    unnamed x4, local copies, waits for them, and re-layouts  2.17 us

profile of v4, /device:TPU:0, one launch (start us, length us, event | category | flops | bytes accessed | tf_op | source)
XLA Modules:
  0.0 43.4 jit_solution(3800331703694748527)
XLA Ops:
  0.6 40.6 %message_round.1 = (bf16[128,256]{1,0:T(8,128)(2,1)}, bf16[256,256]{1,0:T(8,128)(2,1)}) custom-call(bf16[256,256]{1,0:T(8,128)(2,1)} %flow_state_hbm.1, bf16[128,256]{1,0:T(8,128)(2,1)} %link_state_hbm.1, bf16[1,1,24,128,128]{4,3,2,1,0:T(8,128)(2,1)} %coefs_hbm.1, bf16[256,256]{1,0:T(8,128)(2,1)} %link_agg_hbm.1, bf16[256,256]{1,0:T(8,128)(2,1)} %link_self_hbm.1, ...), custom_call_target="tpu_custom_call" | custom-call | tf_op jit(solution)/shard_map/message_round/pallas_call | solution.py:439
  41.3 0.0 copy-start
  41.3 1.5 %copy.18 = bf16[128,256]{1,0:T(8,128)(2,1)} copy(bf16[128,256]{1,0:T(8,128)(2,1)} %get-tuple-element.4) | data formatting | bytes 131072
  42.8 0.0 copy-done
  42.8 0.7 %copy.19 = bf16[256,256]{1,0:T(8,128)(2,1)} copy(bf16[256,256]{1,0:T(8,128)(2,1)S(1)} %copy-done) | data formatting | bytes 262144
Async XLA Ops:
  41.3 1.5 %copy-start = (bf16[256,256]{1,0:T(8,128)(2,1)S(1)}, bf16[256,256]{1,0:T(8,128)(2,1)}, u32[]{:S(2)}) copy-start(bf16[256,256]{1,0:T(8,128)(2,1)} %get-tuple-element.5) | copy-start | bytes 393220

commit v5 on v4

--- a/solution.py
+++ b/solution.py
@@ -439,8 +439,8 @@
     return pl.pallas_call(
         functools.partial(kernel, rows, cols),
         out_shape=(
-            jax.ShapeDtypeStruct(link_state.shape, bf16),
-            jax.ShapeDtypeStruct(flow_state.shape, bf16),
+            pltpu.VMEM(link_state.shape, bf16),
+            pltpu.VMEM(flow_state.shape, bf16),
         ),
         in_specs=[hbm] * 14,
         out_specs=(vmem, vmem),

time: 43.6 us -> 42 us (0.963)
  local copies, waits for them, and re-layouts: 2.17 us -> 1.29 us
  Pallas kernels: 40.6 us -> 39.9 us
    unnamed x4 -> x2, local copies, waits for them, and re-layouts: 2.17 us -> 1.29 us
    pallas_call x1, Pallas kernels: 40.6 us -> 39.9 us  [on_device(): pl.pallas_call(functools.partial(kernel, rows, cols), out_shape=(pltpu.VM...]
where the time goes in v5:
time: 42 us; the launch traced here: 41.9 us
  Pallas kernels  39.9 us (95%)
  local copies, waits for them, and re-layouts  1.29 us (3%)
  between operations  0.64 us (2%)
    pallas_call x1, Pallas kernels, on_device(): pl.pallas_call(functools.partial(kernel, rows, cols), out_shape=(pltpu.VM...  39.9 us
    unnamed x2, local copies, waits for them, and re-layouts  1.29 us

profile of v5, /device:TPU:0, one launch (start us, length us, event | category | flops | bytes accessed | tf_op | source)
XLA Modules:
  0.0 41.9 jit_solution(13219451878581076532)
XLA Ops:
  0.6 39.9 %message_round.1 = (bf16[128,256]{1,0:T(8,128)(2,1)S(1)}, bf16[256,256]{1,0:T(8,128)(2,1)S(1)}) custom-call(bf16[256,256]{1,0:T(8,128)(2,1)} %flow_state_hbm.1, bf16[128,256]{1,0:T(8,128)(2,1)} %link_state_hbm.1, bf16[1,1,24,128,128]{4,3,2,1,0:T(8,128)(2,1)} %coefs_hbm.1, bf16[256,256]{1,0:T(8,128)(2,1)} %link_agg_hbm.1, bf16[256,256]{1,0:T(8,128)(2,1)} %link_self_hbm.1, ...), custom_call_target="tpu_custom_call" | custom-call | tf_op jit(solution)/shard_map/message_round/pallas_call | solution.py:439
  40.6 0.6 %copy.18 = bf16[128,256]{1,0:T(8,128)(2,1)} copy(bf16[128,256]{1,0:T(8,128)(2,1)S(1)} %get-tuple-element.2) | data formatting | bytes 131072
  41.2 0.7 %copy.19 = bf16[256,256]{1,0:T(8,128)(2,1)} copy(bf16[256,256]{1,0:T(8,128)(2,1)S(1)} %get-tuple-element.3) | data formatting | bytes 262144
